TPU v7x, 128 devices: a whole 4x4x4 slice. The times are simulated.
128 devices in a mesh: section: 4 (over z), expert: 32 (over x, y, core).
Axes of the slice: x: 4, y: 4, z: 4, core: 2. Of those that a mesh axis runs over, the one named last changes fastest.
Arguments:
- inputs: bfloat16 [4, 1024, 3584], P(None, 'expert'), may hold values from -5 to 5
- routes: int32 [4, 4, 1024, 2], P('section', None, 'expert'), may hold values from 0 to 7, as said below
- norm_gain: bfloat16 [4, 3584], P('section'), may hold values from 0.099609375 to 1.8984375
- router: bfloat16 [4, 3584, 8], P('section'), may hold values from -0.0234375 to 0.0234375
- w_gate: bfloat16 [4, 3584, 19456], P('section', None, 'expert'), may hold values from -0.09375 to 0.09375
- w_up: bfloat16 [4, 3584, 19456], P('section', None, 'expert'), may hold values from -0.09375 to 0.09375
- w_down: bfloat16 [4, 19456, 3584], P('section', 'expert'), may hold values from -0.25 to 0.25
Outputs:
- outputs: bfloat16 [4, 1024, 3584], P(None, 'expert', 'section')
Inputs may be any that keep to these rules, and one draw needn't show every extreme that they name: `routes`: for each layer and micro-batch, the rows of one index of expert (32 tokens, two choices each) name each expert at most 9 times; a token's two ids differ.
All inputs are finite; a program needn't handle non-finite values.
Results may differ from a plain program's by a relative error of at most 0.024.
Values may be sent and summed in bfloat16 or wider, within the bound.
A program may use at most 128 MiB of HBM per device.

v0:
```python
import jax
import jax.numpy as jnp
from jax import lax
from jax.sharding import PartitionSpec as P

EPSILON = 1e-06


def from_behind(array, axis, by):
    length = lax.axis_size(axis)
    pairs = [(i, i + by) for i in range(length) if 0 <= i + by < length]
    return lax.ppermute(array, axis, pairs)


def normalized(hidden, gain):
    widened = hidden.astype(jnp.float32)
    meansq = jnp.mean(widened * widened, axis=-1, keepdims=True)
    return (
        widened,
        (widened * lax.rsqrt(meansq + EPSILON) * gain.astype(jnp.float32)).astype(jnp.bfloat16),
    )


def expert_block(arrived, gate_block, up_block, down_block):
    gate_part = jnp.dot(arrived, gate_block, preferred_element_type=jnp.float32)
    upward = jnp.dot(arrived, up_block, preferred_element_type=jnp.float32)
    between = (jax.nn.silu(gate_part) * upward).astype(jnp.bfloat16)
    return jnp.dot(between, down_block, preferred_element_type=jnp.float32).astype(jnp.bfloat16)


def expert_pass(flat_choice, flat_rows, capacity, experts_total, weights):
    gate_block, up_block, down_block = weights
    devices_count = lax.axis_size("expert")
    members = devices_count // experts_total
    feature_count = flat_rows.shape[1]
    slots_total = experts_total * capacity
    onehot = (flat_choice[:, None] == jnp.arange(experts_total, dtype=jnp.int32)[None, :]).astype(
        jnp.int32
    )
    before = jnp.cumsum(onehot, axis=0) - onehot
    slot_index = jnp.sum(before * onehot, axis=1)
    target = flat_choice * capacity + slot_index
    placing = (target[:, None] == jnp.arange(slots_total, dtype=jnp.int32)[None, :]).astype(
        jnp.bfloat16
    )
    outgoing = lax.dot_general(
        placing, flat_rows, (((0,), (0,)), ((), ())), preferred_element_type=jnp.float32
    )
    outgoing = outgoing.astype(jnp.bfloat16).reshape(experts_total, capacity, feature_count)
    outgoing = jnp.repeat(outgoing, members, axis=0)
    arrived = lax.all_to_all(outgoing, "expert", split_axis=0, concat_axis=0, tiled=True)
    sources, item_count, width = arrived.shape
    answered = expert_block(
        arrived.reshape(sources * item_count, width), gate_block, up_block, down_block
    )
    answered = answered.reshape(sources, item_count, width)
    came_back = lax.all_to_all(answered, "expert", split_axis=0, concat_axis=0, tiled=True)
    combined = came_back.reshape(experts_total, members, capacity, feature_count).astype(
        jnp.float32
    )
    combined = jnp.sum(combined, axis=1).reshape(slots_total, feature_count)
    return jnp.take(combined, target, axis=0)


def on_device(inputs, routes, norm_gain, router, w_gate, w_up, w_down):
    position = lax.axis_index("section")
    sections = lax.axis_size("section")
    micros, tokens_here, feature_count = inputs.shape
    capacity = tokens_here // 4 + tokens_here // 32
    weights = (w_gate[0], w_up[0], w_down[0])
    gain_row = norm_gain[0]
    columns = router[0]
    experts_total = columns.shape[1]
    expert_range = jnp.arange(experts_total, dtype=jnp.int32)
    is_first = position == 0
    is_last = position == sections - 1
    current = inputs[0]
    finished_all = jnp.zeros_like(inputs)
    steps_total = micros + sections - 1
    for moment in range(steps_total):
        current_micro = jnp.clip(moment - position, 0, micros - 1)
        chosen = lax.dynamic_index_in_dim(routes[0], current_micro, 0, keepdims=False)
        widened, normed = normalized(current, gain_row)
        logits = jnp.dot(normed, columns, preferred_element_type=jnp.float32)
        first_logit = jnp.sum(
            jnp.where(chosen[:, 0:1] == expert_range[None, :], logits, 0.0), axis=1
        )
        second_logit = jnp.sum(
            jnp.where(chosen[:, 1:2] == expert_range[None, :], logits, 0.0), axis=1
        )
        first_weight = jax.nn.sigmoid(first_logit - second_logit)
        second_weight = 1.0 - first_weight
        flat_choice = jnp.concatenate([chosen[:, 0], chosen[:, 1]])
        answers = expert_pass(
            flat_choice, jnp.concatenate([normed, normed], axis=0), capacity, experts_total, weights
        )
        first_out = answers[:tokens_here]
        second_out = answers[tokens_here:]
        updated = (
            widened + first_weight[:, None] * first_out + second_weight[:, None] * second_out
        ).astype(jnp.bfloat16)
        finished = moment - (sections - 1)
        stored = lax.dynamic_update_index_in_dim(
            finished_all, updated, jnp.clip(finished, 0, micros - 1), 0
        )
        finished_all = jnp.where(is_last & (finished >= 0), stored, finished_all)
        if moment + 1 < steps_total:
            passed = from_behind(updated, "section", 1)
            incoming = inputs[moment + 1] if moment + 1 < micros else passed
            current = jnp.where(is_first, incoming, passed)
    share = lax.psum_scatter(
        jnp.where(is_last, finished_all.astype(jnp.float32), 0.0).astype(jnp.bfloat16),
        "section",
        scatter_dimension=2,
        tiled=True,
    )
    return share


def solution(mesh):
    return jax.shard_map(
        on_device,
        mesh=mesh,
        in_specs=(
            P(None, "expert", None),
            P("section", None, "expert", None),
            P("section", None),
            P("section", None, None),
            P("section", None, "expert"),
            P("section", None, "expert"),
            P("section", "expert", None),
        ),
        out_specs=P(None, "expert", "section"),
        check_vma=False,
    )
```

profile of v0, /device:TPU:1, one launch (start us, length us, event | category | flops | bytes accessed | tf_op | source)
XLA Modules:
  0.0 1030.7 jit_solution(16428799962010548866)
XLA Ops:
  12.4 53.8 %all_to_all.70 = bf16[32,9,3584]{2,1,0:T(8,128)(2,1)} all-to-all(bf16[32,9,3584]{2,1,0:T(8,128)(2,1)S(1)} %bitcast.252), channel_id=1, replica_groups=mesh['section'=4,'expert'=32] {'expert'}, dimensions={0} | all-to-all | bytes 4128768 | tf_op jit(solution)/shard_map/all_to_all | solution.py:51
  73.4 9.1 convolution_convert_fusion.6
  93.0 44.4 %all-to-all-done.1 = bf16[32,9,3584]{2,1,0:T(8,128)(2,1)} async-done(((bf16[32,9,3584]{2,1,0:T(8,128)(2,1)}), bf16[32,9,3584]{2,1,0:T(8,128)(2,1)}, u32[]{:S(2)}, u32[]{:S(2)}) %all-to-all-start.1) | async-done | bytes 2064416 | tf_op jit(solution)/shard_map/all_to_all | solution.py:57
  150.8 52.9 %all_to_all.71 = bf16[32,9,3584]{2,1,0:T(8,128)(2,1)} all-to-all(bf16[32,9,3584]{2,1,0:T(8,128)(2,1)S(1)} %bitcast.253), channel_id=1, replica_groups=mesh['section'=4,'expert'=32] {'expert'}, dimensions={0} | all-to-all | bytes 4128768 | tf_op jit(solution)/shard_map/all_to_all | solution.py:51
  208.2 4.6 fusion.31
  212.8 9.7 convolution_convert_fusion.5
  227.0 4.6 all-to-all-start.3
  232.1 45.3 %all-to-all-done.3 = bf16[32,9,3584]{2,1,0:T(8,128)(2,1)} async-done(((bf16[32,9,3584]{2,1,0:T(8,128)(2,1)}), bf16[32,9,3584]{2,1,0:T(8,128)(2,1)}, u32[]{:S(2)}, u32[]{:S(2)}) %all-to-all-start.3) | async-done | bytes 2064416 | tf_op jit(solution)/shard_map/all_to_all | solution.py:57
  292.2 53.0 %all_to_all.72 = bf16[32,9,3584]{2,1,0:T(8,128)(2,1)} all-to-all(bf16[32,9,3584]{2,1,0:T(8,128)(2,1)S(1)} %bitcast.254), channel_id=1, replica_groups=mesh['section'=4,'expert'=32] {'expert'}, dimensions={0} | all-to-all | bytes 4128768 | tf_op jit(solution)/shard_map/all_to_all | solution.py:51
  349.7 4.6 fusion.29
  354.3 9.7 convolution_convert_fusion.4
  373.5 45.4 %all-to-all-done.5 = bf16[32,9,3584]{2,1,0:T(8,128)(2,1)} async-done(((bf16[32,9,3584]{2,1,0:T(8,128)(2,1)}), bf16[32,9,3584]{2,1,0:T(8,128)(2,1)}, u32[]{:S(2)}, u32[]{:S(2)}) %all-to-all-start.5) | async-done | bytes 2064416 | tf_op jit(solution)/shard_map/all_to_all | solution.py:57
  433.7 53.0 %all_to_all.73 = bf16[32,9,3584]{2,1,0:T(8,128)(2,1)} all-to-all(bf16[32,9,3584]{2,1,0:T(8,128)(2,1)S(1)} %bitcast.255), channel_id=1, replica_groups=mesh['section'=4,'expert'=32] {'expert'}, dimensions={0} | all-to-all | bytes 4128768 | tf_op jit(solution)/shard_map/all_to_all | solution.py:51
  491.2 4.6 fusion.27
  495.8 9.7 convolution_convert_fusion.3
  510.0 4.6 all-to-all-start.7
  515.4 45.0 %all-to-all-done.7 = bf16[32,9,3584]{2,1,0:T(8,128)(2,1)} async-done(((bf16[32,9,3584]{2,1,0:T(8,128)(2,1)}), bf16[32,9,3584]{2,1,0:T(8,128)(2,1)}, u32[]{:S(2)}, u32[]{:S(2)}) %all-to-all-start.7) | async-done | bytes 2064416 | tf_op jit(solution)/shard_map/all_to_all | solution.py:57
  574.3 53.3 %all_to_all.74 = bf16[32,9,3584]{2,1,0:T(8,128)(2,1)} all-to-all(bf16[32,9,3584]{2,1,0:T(8,128)(2,1)S(1)} %bitcast.256), channel_id=1, replica_groups=mesh['section'=4,'expert'=32] {'expert'}, dimensions={0} | all-to-all | bytes 4128768 | tf_op jit(solution)/shard_map/all_to_all | solution.py:51
  632.0 4.6 fusion.25
  636.6 9.7 convolution_convert_fusion.2
  650.8 4.6 all-to-all-start.9
  656.8 44.4 %all-to-all-done.9 = bf16[32,9,3584]{2,1,0:T(8,128)(2,1)} async-done(((bf16[32,9,3584]{2,1,0:T(8,128)(2,1)}), bf16[32,9,3584]{2,1,0:T(8,128)(2,1)}, u32[]{:S(2)}, u32[]{:S(2)}) %all-to-all-start.9) | async-done | bytes 2064416 | tf_op jit(solution)/shard_map/all_to_all | solution.py:57
  715.7 53.0 %all_to_all.75 = bf16[32,9,3584]{2,1,0:T(8,128)(2,1)} all-to-all(bf16[32,9,3584]{2,1,0:T(8,128)(2,1)S(1)} %bitcast.257), channel_id=1, replica_groups=mesh['section'=4,'expert'=32] {'expert'}, dimensions={0} | all-to-all | bytes 4128768 | tf_op jit(solution)/shard_map/all_to_all | solution.py:51
  775.9 9.1 convolution_convert_fusion.1
  789.5 4.8 all-to-all-start.11
  794.7 45.3 %all-to-all-done.11 = bf16[32,9,3584]{2,1,0:T(8,128)(2,1)} async-done(((bf16[32,9,3584]{2,1,0:T(8,128)(2,1)}), bf16[32,9,3584]{2,1,0:T(8,128)(2,1)}, u32[]{:S(2)}, u32[]{:S(2)}) %all-to-all-start.11) | async-done | bytes 2064416 | tf_op jit(solution)/shard_map/all_to_all | solution.py:57
  855.5 53.0 %all_to_all.76 = bf16[32,9,3584]{2,1,0:T(8,128)(2,1)} all-to-all(bf16[32,9,3584]{2,1,0:T(8,128)(2,1)S(1)} %bitcast.258), channel_id=1, replica_groups=mesh['section'=4,'expert'=32] {'expert'}, dimensions={0} | all-to-all | bytes 4128768 | tf_op jit(solution)/shard_map/all_to_all | solution.py:51
  913.0 4.7 fusion.21
  917.6 9.7 convolution_convert_fusion
  936.7 45.5 %all-to-all-done.13 = bf16[32,9,3584]{2,1,0:T(8,128)(2,1)} async-done(((bf16[32,9,3584]{2,1,0:T(8,128)(2,1)}), bf16[32,9,3584]{2,1,0:T(8,128)(2,1)}, u32[]{:S(2)}, u32[]{:S(2)}) %all-to-all-start.13) | async-done | bytes 2064416 | tf_op jit(solution)/shard_map/all_to_all | solution.py:57
  990.8 5.5 reshape.572
  996.3 23.8 %reduce-scatter.4.cloned.1.call-done = bf16[896,128]{1,0:T(8,128)(2,1)} async-done(((bf16[3584,128]{1,0:T(8,128)(2,1)}), bf16[896,128]{1,0:T(8,128)(2,1)}) %reduce-scatter.4.cloned.1.call-update) | async-done | bytes 229392
  (196 shorter events, 190.9 us)
Async XLA Ops:
  6.5 85.2 %copy-start = (bf16[1,3584,8]{1,2,0:T(8,128)(2,1)S(1)}, bf16[1,3584,8]{1,2,0:T(8,128)(2,1)}, u32[]{:S(2)}) copy-start(bf16[1,3584,8]{1,2,0:T(8,128)(2,1)} %param.12) | copy-start | bytes 172036
  87.0 50.4 %all-to-all-start.1 = ((bf16[32,9,3584]{2,1,0:T(8,128)(2,1)}), bf16[32,9,3584]{2,1,0:T(8,128)(2,1)}, u32[]{:S(2)}, u32[]{:S(2)}) async-start(bf16[32,9,3584]{2,1,0:T(8,128)(2,1)} %reshape.454), calls=%async_computation.1 | async-start | bytes 7340032 | tf_op jit(solution)/shard_map/all_to_all | solution.py:57
  140.5 1.2 copy-start.2
  141.8 7.6 collective-permute-start
  227.0 50.4 %all-to-all-start.3 = ((bf16[32,9,3584]{2,1,0:T(8,128)(2,1)}), bf16[32,9,3584]{2,1,0:T(8,128)(2,1)}, u32[]{:S(2)}, u32[]{:S(2)}) async-start(bf16[32,9,3584]{2,1,0:T(8,128)(2,1)} %reshape.459), calls=%async_computation.3 | async-start | bytes 7340032 | tf_op jit(solution)/shard_map/all_to_all | solution.py:57
  281.7 8.1 collective-permute-start.1
  368.5 50.4 %all-to-all-start.5 = ((bf16[32,9,3584]{2,1,0:T(8,128)(2,1)}), bf16[32,9,3584]{2,1,0:T(8,128)(2,1)}, u32[]{:S(2)}, u32[]{:S(2)}) async-start(bf16[32,9,3584]{2,1,0:T(8,128)(2,1)} %reshape.464), calls=%async_computation.5 | async-start | bytes 7340032 | tf_op jit(solution)/shard_map/all_to_all | solution.py:57
  423.2 8.2 collective-permute-start.2
  510.0 50.4 %all-to-all-start.7 = ((bf16[32,9,3584]{2,1,0:T(8,128)(2,1)}), bf16[32,9,3584]{2,1,0:T(8,128)(2,1)}, u32[]{:S(2)}, u32[]{:S(2)}) async-start(bf16[32,9,3584]{2,1,0:T(8,128)(2,1)} %reshape.469), calls=%async_computation.7 | async-start | bytes 7340032 | tf_op jit(solution)/shard_map/all_to_all | solution.py:57
  514.7 0.5 copy-start.3
  564.7 8.1 collective-permute-start.3
  650.8 50.4 %all-to-all-start.9 = ((bf16[32,9,3584]{2,1,0:T(8,128)(2,1)}), bf16[32,9,3584]{2,1,0:T(8,128)(2,1)}, u32[]{:S(2)}, u32[]{:S(2)}) async-start(bf16[32,9,3584]{2,1,0:T(8,128)(2,1)} %reshape.474), calls=%async_computation.9 | async-start | bytes 7340032 | tf_op jit(solution)/shard_map/all_to_all | solution.py:57
  706.2 8.1 collective-permute-start.4
  789.4 4.8 copy-start.5
  789.5 5.1 copy-start.4
  789.5 50.6 %all-to-all-start.11 = ((bf16[32,9,3584]{2,1,0:T(8,128)(2,1)}), bf16[32,9,3584]{2,1,0:T(8,128)(2,1)}, u32[]{:S(2)}, u32[]{:S(2)}) async-start(bf16[32,9,3584]{2,1,0:T(8,128)(2,1)} %reshape.479), calls=%async_computation.11 | async-start | bytes 7340032 | tf_op jit(solution)/shard_map/all_to_all | solution.py:57
  846.0 8.1 collective-permute-start.5
  931.8 50.4 %all-to-all-start.13 = ((bf16[32,9,3584]{2,1,0:T(8,128)(2,1)}), bf16[32,9,3584]{2,1,0:T(8,128)(2,1)}, u32[]{:S(2)}, u32[]{:S(2)}) async-start(bf16[32,9,3584]{2,1,0:T(8,128)(2,1)} %reshape.484), calls=%async_computation.13 | async-start | bytes 7340032 | tf_op jit(solution)/shard_map/all_to_all | solution.py:57
  936.4 83.7 %reduce-scatter.4.cloned.1.call-start = ((), (), s32[]{:S(2)}) async-start(), calls=%async_computation.15 | async-start | bytes 1146880
  985.3 1.2 copy-start.1
Sparse Core Ops, SparseCore 0:
  996.4 23.6 reduce-scatter.3
where the time goes:
time: 1040 us; the launch traced here: 1030 us
  blocking collectives  372 us (36%)
  waiting for transfers between devices  362 us (35%)
  matrix products  103 us (10%)
  local copies, waits for them, and re-layouts  87.5 us (8%)
  starting transfers between devices  56.7 us (5%)
  other arithmetic  34.9 us (3%)
  between operations  14.5 us (1%)
    all_to_all x7, blocking collectives, expert_pass(): lax.all_to_all(outgoing, 'expert', split_axis=0, concat_axis=0, tiled=True)  372 us
    all_to_all x7, waiting for transfers between devices, expert_pass(): lax.all_to_all(answered, 'expert', split_axis=0, concat_axis=0, tiled=True)  315 us
    dot_general x7, matrix products, expert_block(): jnp.dot(between, down_block, preferred_element_type=jnp.float32)  66.9 us
    all_to_all x7, starting transfers between devices, expert_pass(): lax.all_to_all(answered, 'expert', split_axis=0, concat_axis=0, tiled=True)  32.5 us
    dot_general x7, matrix products, expert_block(): gate_part = jnp.dot(arrived, gate_block, preferred_element_type=jnp.float32)  31.3 us
    reshape x7, local copies, waits for them, and re-layouts, expert_pass(): answered = answered.reshape(sources, item_count, width)  30.9 us
    reshape x7, local copies, waits for them, and re-layouts, expert_pass(): arrived.reshape(sources * item_count, width)  28.7 us
    ppermute x6, starting transfers between devices, from_behind(): return lax.ppermute(array, axis, pairs)  24.1 us
  transfers between devices with their start and end apart: 14, of which 14 were waited for; matrix products, arithmetic and copies ran while one was open for 1% of the time, Pallas kernels for 0%

commit v1 on v0

v1 whole, which is shorter than its diff:
```python
import functools

import numpy as np
import jax
import jax.numpy as jnp
from jax import lax
from jax.experimental import pallas as pl
from jax.experimental.pallas import tpu as pltpu
from jax.sharding import PartitionSpec as P

EPSILON = 1e-06
MESH = pl.DeviceIdType.MESH
F32 = jnp.float32
BF16 = jnp.bfloat16

CAP = 9
WIDE = 512
PIECES = 7
BLOCK = 64
SOURCES = 8
PACKED = 80
CHIPS = 16


def selection():
    table = np.zeros((PIECES * PACKED, SOURCES * BLOCK), np.float32)
    for piece in range(PIECES):
        for source in range(SOURCES):
            for slot in range(CAP):
                table[
                    piece * PACKED + source * CAP + slot, source * BLOCK + piece * CAP + slot
                ] = 1.0
    return table


def kernel(
    inputs, routes, routes_row, gain, router, gate_in, up_in, down_in, sel, unsel,
    out,
    w_gate, w_up, w_down, hid, d_out, held, packed, answers, own_sum, sib_out, sib_in,
    ret_out, came, weight_hi, weight_lo, h_out,
    w_sem, h_sem, d_sem, sib_sem, ret_sem, out_sem,
    d_sent, f_sent, sib_sent, ret_sent, h_sent,
):
    micros, tokens, _ = inputs.shape
    units = 2 * micros
    section = lax.axis_index("section")
    place = lax.axis_index("expert")
    sections = 4
    core = lax.rem(place, 2)
    chip = place // 2
    side = chip // 8
    sibling = (section, chip * 2 + (1 - core))

    weight_copies = [
        pltpu.make_async_copy(gate_in, w_gate, w_sem.at[0]),
        pltpu.make_async_copy(up_in, w_up, w_sem.at[1]),
        pltpu.make_async_copy(down_in, w_down, w_sem.at[2]),
    ]

    def input_copy(m):
        return pltpu.make_async_copy(inputs.at[m], hid.at[m], h_sem.at[m])

    def relay_copy(m):
        return pltpu.make_async_remote_copy(
            h_out.at[m], hid.at[m], h_sent, h_sem.at[m],
            device_id=(lax.rem(section + 1, sections), place), device_id_type=MESH,
        )

    @pl.when(section == 0)
    def _():
        for m in range(micros):
            input_copy(m).start()

    barrier = pltpu.get_barrier_semaphore()

    def greet(step, carry):
        pl.semaphore_signal(
            barrier, inc=1, device_id=(section, lax.rem(place + step, 32)), device_id_type=MESH
        )
        return carry

    lax.fori_loop(1, 32, greet, 0)
    for step in range(1, sections):
        pl.semaphore_signal(
            barrier, inc=1, device_id=(lax.rem(section + step, sections), place),
            device_id_type=MESH,
        )
    for copy in weight_copies:
        copy.start()
    pl.semaphore_wait(barrier, 31 + sections - 1)

    def dispatch_copy(m, expert, to, source):
        return pltpu.make_async_remote_copy(
            d_out.at[m, pl.ds(pl.multiple_of(expert * BLOCK, BLOCK), BLOCK)],
            held.at[2 * m + core, source],
            d_sent, d_sem.at[2 * m + core, source],
            device_id=(section, to * 2 + side), device_id_type=MESH,
        )

    def dispatch_stay(m):
        return pltpu.make_async_copy(
            d_out.at[m, pl.ds(pl.multiple_of((chip // 2) * BLOCK, BLOCK), BLOCK)],
            held.at[2 * m + core, chip], d_sem.at[2 * m + core, chip],
        )

    def dispatch(m):
        input_copy(m).wait()
        hidden = hid[m].astype(F32)
        meansq = jnp.mean(hidden * hidden, axis=-1, keepdims=True)
        normed = (hidden * lax.rsqrt(meansq + EPSILON) * gain[...].astype(F32)).astype(BF16)
        stacked = jnp.concatenate(
            [normed[:, k * WIDE:(k + 1) * WIDE] for k in range(PIECES)], axis=0
        )
        chosen = routes[m]
        first, second = chosen[:, 0:1], chosen[:, 1:2]
        along = routes_row[m]
        first_row, second_row = along[0:1], along[1:2]
        width = PIECES * tokens
        up_down = lax.broadcasted_iota(jnp.int32, (tokens, width), 0)
        left_right = lax.broadcasted_iota(jnp.int32, (tokens, width), 1)
        token_of = lax.rem(left_right, tokens)
        earlier = up_down < token_of

        def total(condition, axis):
            return jnp.sum(jnp.where(condition, 1, 0), axis=axis, keepdims=True)

        slot_first = total((first == first_row) & earlier, 0)
        slot_second = total(first == second_row, 0) + total((second == second_row) & earlier, 0)
        piece_row = lax.broadcasted_iota(jnp.int32, (1, width), 1) // tokens * CAP
        target_first = first_row * BLOCK + piece_row + slot_first
        target_second = second_row * BLOCK + piece_row + slot_second
        rows = lax.broadcasted_iota(jnp.int32, (8 * BLOCK, width), 0)
        placing = jnp.where((rows == target_first) | (rows == target_second), 1.0, 0.0)
        outgoing = jnp.dot(placing.astype(BF16), stacked, preferred_element_type=F32)
        d_out[m] = outgoing.astype(BF16)

        def send(step, carry):
            to = lax.rem(chip + step, CHIPS)
            dispatch_copy(m, to // 2, to, chip).start()
            return carry

        lax.fori_loop(1, CHIPS, send, 0)

        @pl.when(side == core)
        def _():
            dispatch_stay(m).start()

        @pl.when(side != core)
        def _():
            dispatch_copy(m, chip // 2, chip, chip).start()

        logits = jnp.dot(normed, router[...], preferred_element_type=F32)
        expert_range = lax.broadcasted_iota(jnp.int32, logits.shape, 1)
        first_logit = jnp.sum(jnp.where(first == expert_range, logits, 0.0), axis=1, keepdims=True)
        second_logit = jnp.sum(
            jnp.where(second == expert_range, logits, 0.0), axis=1, keepdims=True
        )
        first_weight = 1.0 / (1.0 + jnp.exp(second_logit - first_logit))
        second_weight = 1.0 - first_weight
        before = (left_right < up_down) & (left_right < tokens)
        own_first = total((first == first_row) & before, 1)
        own_second = total((second == first_row) & (left_right < tokens), 1) + total(
            (second == second_row) & before, 1
        )
        at_first = first * BLOCK + own_first
        at_second = second * BLOCK + own_second
        column = lax.broadcasted_iota(jnp.int32, (tokens, CHIPS * BLOCK), 1)
        column = column // (2 * BLOCK) * BLOCK + lax.rem(column, BLOCK)
        for k in range(PIECES):
            weights = jnp.where(column == at_first + k * CAP, first_weight, 0.0) + jnp.where(
                column == at_second + k * CAP, second_weight, 0.0
            )
            high = weights.astype(BF16)
            weight_hi[k * tokens:(k + 1) * tokens, :] = high
            weight_lo[k * tokens:(k + 1) * tokens, :] = (weights - high.astype(F32)).astype(BF16)

    def block_arrival(u, source):
        return pltpu.make_async_copy(
            held.at[u, source], held.at[u, source], d_sem.at[u, source]
        )

    def forward_copy(u, source):
        return pltpu.make_async_remote_copy(
            held.at[u, source], held.at[u, source], f_sent, d_sem.at[u, source],
            device_id=sibling, device_id_type=MESH,
        )

    def sibling_copy(u):
        return pltpu.make_async_remote_copy(
            sib_out.at[u], sib_in.at[u], sib_sent, sib_sem.at[u],
            device_id=sibling, device_id_type=MESH,
        )

    def return_copy(u, k):
        home = core * SOURCES + k
        return pltpu.make_async_remote_copy(
            ret_out.at[u, k], came.at[u // 2, chip], ret_sent, ret_sem.at[u // 2, chip],
            device_id=(section, home * 2 + lax.rem(u, 2)), device_id_type=MESH,
        )

    def return_stay(u, k):
        return pltpu.make_async_copy(
            ret_out.at[u, k], came.at[u // 2, chip], ret_sem.at[u // 2, chip]
        )

    def stays(u, k):
        return (core * SOURCES + k == chip) & (lax.rem(u, 2) == core)

    def select(u, base):
        blocks = held[u, pl.ds(base, SOURCES)].reshape(SOURCES * BLOCK, WIDE)
        return jnp.dot(sel[...], blocks, preferred_element_type=F32).astype(BF16)

    def compute(u):
        own, other = core * SOURCES, (1 - core) * SOURCES

        def pass_on(k, carry):
            block_arrival(u, own + k).wait()
            forward_copy(u, own + k).start()
            return carry

        lax.fori_loop(0, SOURCES, pass_on, 0)
        mine = select(u, own)
        for k in range(PIECES):
            packed[0:PACKED, k * WIDE:(k + 1) * WIDE] = mine[k * PACKED:(k + 1) * PACKED]

        def arrive(k, carry):
            block_arrival(u, other + k).wait()
            return carry

        lax.fori_loop(0, SOURCES, arrive, 0)
        theirs = select(u, other)
        for k in range(PIECES):
            packed[PACKED:, k * WIDE:(k + 1) * WIDE] = theirs[k * PACKED:(k + 1) * PACKED]
        rows = packed[...]
        gated = jnp.dot(rows, w_gate[...], preferred_element_type=F32)
        upward = jnp.dot(rows, w_up[...], preferred_element_type=F32)
        between = (gated / (1.0 + jnp.exp(-gated)) * upward).astype(BF16)
        for k in range(PIECES):
            part = jnp.dot(
                between, w_down[:, k * WIDE:(k + 1) * WIDE], preferred_element_type=F32
            ).astype(BF16)
            answers[0, k * PACKED:(k + 1) * PACKED] = part[:PACKED]
            answers[1, k * PACKED:(k + 1) * PACKED] = part[PACKED:]
        sib_out[u] = jnp.dot(unsel[...], answers[1], preferred_element_type=F32).astype(BF16)
        sibling_copy(u).start()
        own_sum[...] = jnp.dot(unsel[...], answers[0], preferred_element_type=F32)
        sibling_copy(u).wait_recv()
        summed = (own_sum[...] + sib_in[u].astype(F32)).astype(BF16)
        ret_out[u] = summed.reshape(SOURCES, BLOCK, WIDE)

        def send(k, carry):
            @pl.when(stays(u, k))
            def _():
                return_stay(u, k).start()

            @pl.when(jnp.logical_not(stays(u, k)))
            def _():
                return_copy(u, k).start()

            return carry

        lax.fori_loop(0, SOURCES, send, 0)

    def out_copy(m, to):
        return pltpu.make_async_remote_copy(
            h_out.at[m, :, to * 896:(to + 1) * 896], out.at[m], h_sent, out_sem.at[m],
            device_id=(to, place), device_id_type=MESH,
        )

    def out_stay(m):
        return pltpu.make_async_copy(
            h_out.at[m, :, 3 * 896:4 * 896], out.at[m], out_sem.at[m]
        )

    def combine(m):
        def arrive(k, carry):
            pltpu.make_async_copy(came.at[m, k], came.at[m, k], ret_sem.at[m, k]).wait()
            return carry

        lax.fori_loop(0, CHIPS, arrive, 0)
        answered = came[m].reshape(CHIPS * BLOCK, WIDE)
        added = jnp.dot(weight_hi[...], answered, preferred_element_type=F32) + jnp.dot(
            weight_lo[...], answered, preferred_element_type=F32
        )
        for k in range(PIECES):
            at = slice(k * WIDE, (k + 1) * WIDE)
            h_out[m, :, at] = (
                hid[m, :, at].astype(F32) + added[k * tokens:(k + 1) * tokens]
            ).astype(BF16)

        @pl.when(section < sections - 1)
        def _():
            relay_copy(m).start()

        @pl.when(section == sections - 1)
        def _():
            for to in range(sections - 1):
                out_copy(m, to).start()
            out_stay(m).start()

    @pl.when(core == 0)
    def _():
        dispatch(0)

    for copy in weight_copies:
        copy.wait()

    def step(u, carry):
        compute(u)

        @pl.when((lax.rem(u + 1, 2) == core) & (u + 1 < units))
        def _():
            dispatch((u + 1) // 2)

        @pl.when(lax.rem(u, 2) == core)
        def _():
            combine(u // 2)

        return carry

    lax.fori_loop(0, units, step, 0)

    def drain(m, carry):
        def drain_dispatch(step, inner):
            to = lax.rem(chip + step, CHIPS)
            dispatch_copy(m, to // 2, to, chip).wait_send()
            return inner

        lax.fori_loop(1, CHIPS, drain_dispatch, 0)

        @pl.when(side != core)
        def _():
            dispatch_copy(m, chip // 2, chip, chip).wait_send()

        for half in range(2):
            u = 2 * m + half
            sibling_copy(u).wait_send()

            def drain_unit(k, inner):
                forward_copy(u, core * SOURCES + k).wait_send()

                @pl.when(jnp.logical_not(stays(u, k)))
                def _():
                    return_copy(u, k).wait_send()

                return inner

            lax.fori_loop(0, SOURCES, drain_unit, 0)

        @pl.when(section < sections - 1)
        def _():
            relay_copy(m).wait_send()

        @pl.when(section == sections - 1)
        def _():
            for to in range(sections - 1):
                out_copy(m, to).wait_send()

        out_stay(m).wait()
        return carry

    lax.fori_loop(0, micros, drain, 0)


def on_device(inputs, routes, norm_gain, router, w_gate, w_up, w_down):
    micros, tokens, features = inputs.shape
    units = 2 * micros
    hidden_units = w_gate.shape[2]
    table = selection()
    sel = jnp.asarray(table, BF16)
    unsel = jnp.asarray(table.T, BF16)
    routes_row = jnp.tile(jnp.swapaxes(routes[0], 1, 2), (1, 1, PIECES))
    vmem = pl.BlockSpec(memory_space=pltpu.VMEM)
    anywhere = pl.BlockSpec(memory_space=pl.ANY)
    dma = pltpu.SemaphoreType.DMA
    return pl.pallas_call(
        kernel,
        out_shape=jax.ShapeDtypeStruct((micros, tokens, features // 4), BF16),
        in_specs=[anywhere, vmem, vmem, vmem, vmem, anywhere, anywhere, anywhere, vmem, vmem],
        out_specs=vmem,
        scratch_shapes=[
            pltpu.VMEM((features, hidden_units), BF16),
            pltpu.VMEM((features, hidden_units), BF16),
            pltpu.VMEM((hidden_units, features), BF16),
            pltpu.VMEM((micros, tokens, features), BF16),
            pltpu.VMEM((micros, 8 * BLOCK, WIDE), BF16),
            pltpu.VMEM((units, CHIPS, BLOCK, WIDE), BF16),
            pltpu.VMEM((2 * PACKED, features), BF16),
            pltpu.VMEM((2, PIECES * PACKED, WIDE), BF16),
            pltpu.VMEM((SOURCES * BLOCK, WIDE), F32),
            pltpu.VMEM((units, SOURCES * BLOCK, WIDE), BF16),
            pltpu.VMEM((units, SOURCES * BLOCK, WIDE), BF16),
            pltpu.VMEM((units, SOURCES, BLOCK, WIDE), BF16),
            pltpu.VMEM((micros, CHIPS, BLOCK, WIDE), BF16),
            pltpu.VMEM((PIECES * tokens, CHIPS * BLOCK), BF16),
            pltpu.VMEM((PIECES * tokens, CHIPS * BLOCK), BF16),
            pltpu.VMEM((micros, tokens, features), BF16),
            dma((3,)),
            dma((micros,)),
            dma((units, CHIPS)),
            dma((units,)),
            dma((micros, CHIPS)),
            dma((micros,)),
            dma, dma, dma, dma, dma,
        ],
        compiler_params=pltpu.CompilerParams(
            collective_id=0, has_side_effects=True, vmem_limit_bytes=60 * 2**20
        ),
        name="moe_relay",
    )(
        inputs, routes[0], routes_row, norm_gain, router[0], w_gate[0], w_up[0], w_down[0],
        sel, unsel,
    )


def solution(mesh):
    return jax.shard_map(
        on_device,
        mesh=mesh,
        in_specs=(
            P(None, "expert", None),
            P("section", None, "expert", None),
            P("section", None),
            P("section", None, None),
            P("section", None, "expert"),
            P("section", None, "expert"),
            P("section", "expert", None),
        ),
        out_specs=P(None, "expert", "section"),
        check_vma=False,
    )
```

time: 1040 us -> 328 us (0.32)
  blocking collectives: 372 us -> 0 us
  waiting for transfers between devices: 362 us -> 0 us
  Pallas kernels: 0 us -> 308 us
  matrix products: 103 us -> 0 us
  local copies, waits for them, and re-layouts: 87.5 us -> 19.6 us
  starting transfers between devices: 56.7 us -> 0 us
  other arithmetic: 34.9 us -> 0 us
  between operations: 14.5 us -> 0.02 us
    all_to_all x7 -> x0, blocking collectives: 372 us -> none  [expert_pass(): lax.all_to_all(outgoing, 'expert', split_axis=0, concat_axis=0, tiled=True)]
    all_to_all x7 -> x0, waiting for transfers between devices: 315 us -> none  [expert_pass(): lax.all_to_all(answered, 'expert', split_axis=0, concat_axis=0, tiled=True)]
    pallas_call x0 -> x1, Pallas kernels: none -> 308 us  [on_device(): pl.pallas_call(kernel, out_shape=jax.ShapeDtypeStruct((micros, tokens, fe...]
    dot_general x28 -> x0, matrix products: 103 us -> none  [the longest x7 66.9 us: expert_block(): jnp.dot(between, down_block, preferred_element_type=jnp.float32)]
    reshape x28 -> x0, local copies, waits for them, and re-layouts: 62.4 us -> none  [the longest x7 30.9 us: expert_pass(): answered = answered.reshape(sources, item_count, width)]
    all_to_all x7 -> x0, starting transfers between devices: 32.5 us -> none  [expert_pass(): lax.all_to_all(answered, 'expert', split_axis=0, concat_axis=0, tiled=True)]
    reduce_sum x21 -> x0, other arithmetic: 25.8 us -> none  [the longest x7 20.5 us: expert_pass(): combined = jnp.sum(combined, axis=1).reshape(slots_total, feature_count)]
    ppermute x6 -> x0, starting transfers between devices: 24.1 us -> none  [from_behind(): return lax.ppermute(array, axis, pairs)]
  transfers between devices with their start and end apart: 14 -> 0, of which waited for: 14 -> 0; matrix products, arithmetic and copies ran while one was open for 1% -> 0% of each run, Pallas kernels for 0% -> 0%
where the time goes in v1:
time: 328 us; the launch traced here: 327 us
  Pallas kernels  308 us (94%)
  local copies, waits for them, and re-layouts  19.6 us (6%)
    pallas_call x1, Pallas kernels, on_device(): pl.pallas_call(kernel, out_shape=jax.ShapeDtypeStruct((micros, tokens, fe...  308 us
    unnamed x7, local copies, waits for them, and re-layouts  18.8 us

profile of v1, /device:TPU:1, one launch (start us, length us, event | category | flops | bytes accessed | tf_op | source)
XLA Modules:
  0.0 327.1 jit_solution(12081719378952859166)
XLA Ops:
  0.0 0.8 copy.15
  0.8 0.0 copy-start
  0.8 0.1 copy.16
  0.9 0.7 tile.10.routes_row
  1.6 2.1 copy.17
  3.6 7.1 %copy.18 = bf16[1,3584,608]{2,1,0:T(8,128)(2,1)} copy(bf16[1,3584,608]{1,2,0:T(8,128)(2,1)} %param.13) | data formatting | bytes 8716288 | tf_op args[4]
  10.8 0.0 copy-done
  10.8 7.2 %copy.19 = bf16[1,3584,608]{2,1,0:T(8,128)(2,1)} copy(bf16[1,3584,608]{1,2,0:T(8,128)(2,1)} %param.14) | data formatting | bytes 8716288 | tf_op args[5]
  17.9 307.5 %moe_relay.1 = bf16[4,32,896]{2,1,0:T(8,128)(2,1)} custom-call(bf16[4,32,3584]{2,1,0:T(8,128)(2,1)} %inputs.1, s32[4,32,2]{2,1,0:T(8,128)} %bitcast.12, s32[4,2,224]{2,1,0:T(2,128)} %tile.10.routes_row, bf16[1,3584]{1,0:T(2,128)(2,1)} %gain.1, bf16[3584,8]{1,0:T(8,128)(2,1)} %bitcast.10, bf16[3584,608]{1,0:T(8,128)(2,1)} %bitcast.7, ...), custom_call_target="tpu_custom_call" | custom-call | tf_op jit(solution)/shard_map/moe_relay/pallas_call | solution.py:376
  325.5 1.6 copy.21
  (1 shorter events, 0.0 us)
Async XLA Ops:
  0.8 10.0 %copy-start = (s32[1,4,32,2]{3,2,1,0:T(8,128)}, s32[1,4,32,2]{3,2,1,0:T(8,128)S(1)}, u32[]{:S(2)}) copy-start(s32[1,4,32,2]{3,2,1,0:T(8,128)S(1)} %copy.15) | copy-start | bytes 3076

commit v2 on v1

v2 whole, which is shorter than its diff:
```python
import jax
import jax.numpy as jnp
from jax import lax
from jax.experimental import pallas as pl
from jax.experimental.pallas import tpu as pltpu
from jax.sharding import PartitionSpec as P

EPSILON = 1e-06
MESH = pl.DeviceIdType.MESH
F32 = jnp.float32
BF16 = jnp.bfloat16

CAP = 9
WIDE = 512
PIECES = 7
HALF = 1792
NARROW = 256
BLOCK = 64
SOURCES = 8
PACKED = 80
CHIPS = 16
AHEAD = 2
BEHIND = 1


def fill_selection(sel, unsel):
    down = lax.broadcasted_iota(jnp.int32, (PIECES * PACKED, 1), 0)
    piece, rest = down // PACKED, lax.rem(down, PACKED)
    source, slot = rest // CAP, lax.rem(rest, CAP)
    taken = jnp.where(rest < SOURCES * CAP, source * BLOCK + piece * CAP + slot, -1)
    sel[...] = jnp.where(
        lax.broadcasted_iota(jnp.int32, sel.shape, 1) == taken, 1.0, 0.0
    ).astype(BF16)
    down = lax.broadcasted_iota(jnp.int32, (SOURCES * BLOCK, 1), 0)
    source, rest = down // BLOCK, lax.rem(down, BLOCK)
    piece, slot = rest // CAP, lax.rem(rest, CAP)
    taken = jnp.where(piece < PIECES, piece * PACKED + source * CAP + slot, -1)
    unsel[...] = jnp.where(
        lax.broadcasted_iota(jnp.int32, unsel.shape, 1) == taken, 1.0, 0.0
    ).astype(BF16)


def dot_nt(rows, columns):
    return lax.dot_general(
        rows, columns, (((1,), (1,)), ((), ())), preferred_element_type=F32
    )


def kernel(
    inputs, routes, gain, router, gate_in, up_in, down_in,
    out,
    w_gate, w_up, w_down, sel, unsel, hid, placing, d_out, held, packed, mid_out, mid_in, partial,
    answers, ret_out, came, weight_hi, weight_lo, h_out,
    w_sem, h_sem, d_sem, mid_sem, ret_sem, out_sem,
    swap_sent, d_sent, f_sent, mid_sent, ret_sent, h_sent,
):
    micros, tokens, _ = inputs.shape
    units = 2 * micros
    section = lax.axis_index("section")
    place = lax.axis_index("expert")
    sections = 4
    core = lax.rem(place, 2)
    chip = place // 2
    side = chip // 8
    sibling = (section, chip * 2 + (1 - core))

    def down_half(half):
        return down_in.at[:, pl.ds(pl.multiple_of(half * HALF, HALF), HALF)]

    swap_copy = pltpu.make_async_remote_copy(
        down_half(1 - core), w_down.at[1], swap_sent, w_sem.at[3],
        device_id=sibling, device_id_type=MESH,
    )
    weight_copies = [
        pltpu.make_async_copy(gate_in, w_gate, w_sem.at[0]),
        pltpu.make_async_copy(up_in, w_up, w_sem.at[1]),
        pltpu.make_async_copy(down_half(core), w_down.at[0], w_sem.at[2]),
    ]

    def input_copy(m):
        return pltpu.make_async_copy(inputs.at[m], hid.at[m], h_sem.at[m])

    def relay_copy(m, half):
        at = slice(half * HALF, (half + 1) * HALF)
        return pltpu.make_async_remote_copy(
            h_out.at[m, :, at], hid.at[m, :, at], h_sent, h_sem.at[m],
            device_id=(lax.rem(section + 1, sections), place), device_id_type=MESH,
        )

    @pl.when(section == 0)
    def _():
        for m in range(micros):
            input_copy(m).start()

    barrier = pltpu.get_barrier_semaphore()

    def greet(step, carry):
        pl.semaphore_signal(
            barrier, inc=1, device_id=(section, lax.rem(place + step, 32)), device_id_type=MESH
        )
        return carry

    lax.fori_loop(1, 32, greet, 0)
    for step in range(1, sections):
        pl.semaphore_signal(
            barrier, inc=1, device_id=(lax.rem(section + step, sections), place),
            device_id_type=MESH,
        )
    for copy in weight_copies:
        copy.start()
    fill_selection(sel, unsel)
    pl.semaphore_wait(barrier, 31 + sections - 1)
    swap_copy.start()

    def dispatch_copy(m, expert, to, source):
        return pltpu.make_async_remote_copy(
            d_out.at[m, pl.ds(pl.multiple_of(expert * BLOCK, BLOCK), BLOCK)],
            held.at[2 * m + core, source],
            d_sent, d_sem.at[2 * m + core, source],
            device_id=(section, to * 2 + side), device_id_type=MESH,
        )

    def dispatch_stay(m):
        return pltpu.make_async_copy(
            d_out.at[m, pl.ds(pl.multiple_of((chip // 2) * BLOCK, BLOCK), BLOCK)],
            held.at[2 * m + core, chip], d_sem.at[2 * m + core, chip],
        )

    def dispatch(m):
        width = PIECES * tokens
        up_down = lax.broadcasted_iota(jnp.int32, (tokens, width), 0)
        left_right = lax.broadcasted_iota(jnp.int32, (tokens, width), 1)
        token_of = lax.rem(left_right, tokens)
        chosen = routes[m]
        square = up_down[:, :tokens] == left_right[:, :tokens]
        first = jnp.sum(jnp.where(square, chosen[0:1], 0), axis=1, keepdims=True)
        second = jnp.sum(jnp.where(square, chosen[1:2], 0), axis=1, keepdims=True)
        repeat = up_down == token_of
        first_row = jnp.sum(jnp.where(repeat, first, 0), axis=0, keepdims=True)
        second_row = jnp.sum(jnp.where(repeat, second, 0), axis=0, keepdims=True)
        earlier = up_down < token_of

        def total(condition, axis):
            return jnp.sum(jnp.where(condition, 1, 0), axis=axis, keepdims=True)

        slot_first = total((first == first_row) & earlier, 0)
        slot_second = total(first == second_row, 0) + total((second == second_row) & earlier, 0)
        piece_row = lax.broadcasted_iota(jnp.int32, (1, width), 1) // tokens * CAP
        target_first = first_row * BLOCK + piece_row + slot_first
        target_second = second_row * BLOCK + piece_row + slot_second
        rows = lax.broadcasted_iota(jnp.int32, (8 * BLOCK, width), 0)
        placing[...] = jnp.where(
            (rows == target_first) | (rows == target_second), 1.0, 0.0
        ).astype(BF16)

        input_copy(m).wait()
        hidden = hid[m].astype(F32)
        meansq = jnp.mean(hidden * hidden, axis=-1, keepdims=True)
        normed = (hidden * lax.rsqrt(meansq + EPSILON) * gain[...].astype(F32)).astype(BF16)
        stacked = jnp.concatenate(
            [normed[:, k * WIDE:(k + 1) * WIDE] for k in range(PIECES)], axis=0
        )
        d_out[m] = jnp.dot(placing[...], stacked, preferred_element_type=F32).astype(BF16)

        def send(step, carry):
            to = lax.rem(chip + step, CHIPS)
            dispatch_copy(m, to // 2, to, chip).start()
            return carry

        lax.fori_loop(1, CHIPS, send, 0)

        @pl.when(side == core)
        def _():
            dispatch_stay(m).start()

        @pl.when(side != core)
        def _():
            dispatch_copy(m, chip // 2, chip, chip).start()

        logits = dot_nt(normed, router[...])
        expert_range = lax.broadcasted_iota(jnp.int32, logits.shape, 1)
        first_logit = jnp.sum(jnp.where(first == expert_range, logits, 0.0), axis=1, keepdims=True)
        second_logit = jnp.sum(
            jnp.where(second == expert_range, logits, 0.0), axis=1, keepdims=True
        )
        first_weight = 1.0 / (1.0 + jnp.exp(second_logit - first_logit))
        second_weight = 1.0 - first_weight
        before = (left_right < up_down) & (left_right < tokens)
        own_first = total((first == first_row) & before, 1)
        own_second = total((second == first_row) & (left_right < tokens), 1) + total(
            (second == second_row) & before, 1
        )
        at_first = first * BLOCK + own_first
        at_second = second * BLOCK + own_second
        column = lax.broadcasted_iota(jnp.int32, (tokens, CHIPS * BLOCK), 1)
        column = column // (2 * BLOCK) * BLOCK + lax.rem(column, BLOCK)
        for k in range(PIECES):
            weights = jnp.where(column == at_first + k * CAP, first_weight, 0.0) + jnp.where(
                column == at_second + k * CAP, second_weight, 0.0
            )
            high = weights.astype(BF16)
            weight_hi[lax.rem(m, 2), k * tokens:(k + 1) * tokens] = high
            weight_lo[lax.rem(m, 2), k * tokens:(k + 1) * tokens] = (
                weights - high.astype(F32)
            ).astype(BF16)

    def block_arrival(u, source):
        return pltpu.make_async_copy(
            held.at[u, source], held.at[u, source], d_sem.at[u, source]
        )

    def forward_copy(u, source):
        return pltpu.make_async_remote_copy(
            held.at[u, source], held.at[u, source], f_sent, d_sem.at[u, source],
            device_id=sibling, device_id_type=MESH,
        )

    def between_copy(u, half):
        there, here = slice(half * PACKED, (half + 1) * PACKED), slice(
            (1 - half) * PACKED, (2 - half) * PACKED
        )
        return pltpu.make_async_remote_copy(
            mid_out.at[u, there], mid_in.at[u, here], mid_sent, mid_sem.at[u],
            device_id=sibling, device_id_type=MESH,
        )

    def between_arrival(u):
        return pltpu.make_async_copy(mid_in.at[u], mid_in.at[u], mid_sem.at[u])

    def return_copy(u, home):
        return pltpu.make_async_remote_copy(
            ret_out.at[u, home], came.at[u // 2, core, chip], ret_sent,
            ret_sem.at[u // 2, core, chip],
            device_id=(section, home * 2 + lax.rem(u, 2)), device_id_type=MESH,
        )

    def return_stay(u):
        return pltpu.make_async_copy(
            ret_out.at[u, chip], came.at[u // 2, core, chip], ret_sem.at[u // 2, core, chip]
        )

    def stays(u, home):
        return (home == chip) & (lax.rem(u, 2) == core)

    def select(u, base):
        blocks = held[u, pl.ds(base, SOURCES)].reshape(SOURCES * BLOCK, WIDE)
        return jnp.dot(sel[...], blocks, preferred_element_type=F32).astype(BF16)

    def compute(u):
        own, other = core * SOURCES, (1 - core) * SOURCES

        def pass_on(k, carry):
            block_arrival(u, own + k).wait()
            forward_copy(u, own + k).start()
            return carry

        lax.fori_loop(0, SOURCES, pass_on, 0)
        mine = select(u, own)
        for k in range(PIECES):
            packed[0:PACKED, k * WIDE:(k + 1) * WIDE] = mine[k * PACKED:(k + 1) * PACKED]

        def arrive(k, carry):
            block_arrival(u, other + k).wait()
            return carry

        lax.fori_loop(0, SOURCES, arrive, 0)
        theirs = select(u, other)
        for k in range(PIECES):
            packed[PACKED:, k * WIDE:(k + 1) * WIDE] = theirs[k * PACKED:(k + 1) * PACKED]
        rows = packed[...]
        gated = dot_nt(rows, w_gate[...])
        upward = dot_nt(rows, w_up[...])
        between = (gated / (1.0 + jnp.exp(-gated)) * upward).astype(BF16)
        mid_out[u] = between
        for half in range(2):
            between_copy(u, half).start()
        partial[...] = jnp.dot(between, w_down[0], preferred_element_type=F32)
        between_arrival(u).wait()
        theirs = mid_in[u]
        for k in range(PIECES):
            at = slice(k * NARROW, (k + 1) * NARROW)
            part = partial[:, at] + jnp.dot(
                theirs, w_down[1, :, at], preferred_element_type=F32
            )
            part = part.astype(BF16)
            answers[0, k * PACKED:(k + 1) * PACKED] = part[:PACKED]
            answers[1, k * PACKED:(k + 1) * PACKED] = part[PACKED:]
        for group, base in ((0, own), (1, other)):
            blocks = jnp.dot(unsel[...], answers[group], preferred_element_type=F32)
            ret_out[u, pl.ds(base, SOURCES)] = blocks.astype(BF16).reshape(
                SOURCES, BLOCK, NARROW
            )

            def send(k, carry, base=base):
                home = base + lax.rem(chip + k, SOURCES)

                @pl.when(stays(u, home))
                def _():
                    return_stay(u).start()

                @pl.when(jnp.logical_not(stays(u, home)))
                def _():
                    return_copy(u, home).start()

                return carry

            lax.fori_loop(0, SOURCES, send, 0)

    def out_copy(m, to):
        return pltpu.make_async_remote_copy(
            h_out.at[m, :, to * 896:(to + 1) * 896], out.at[m], h_sent, out_sem.at[m],
            device_id=(to, place), device_id_type=MESH,
        )

    def out_stay(m):
        return pltpu.make_async_copy(
            h_out.at[m, :, 3 * 896:4 * 896], out.at[m], out_sem.at[m]
        )

    def combine(m):
        for half in range(2):
            def arrive(k, carry, half=half):
                pltpu.make_async_copy(
                    came.at[m, half, k], came.at[m, half, k], ret_sem.at[m, half, k]
                ).wait()
                return carry

            lax.fori_loop(0, CHIPS, arrive, 0)
            answered = came[m, half].reshape(CHIPS * BLOCK, NARROW)
            slot = lax.rem(m, 2)
            added = jnp.dot(weight_hi[slot], answered, preferred_element_type=F32) + jnp.dot(
                weight_lo[slot], answered, preferred_element_type=F32
            )
            for k in range(PIECES):
                at = slice(half * HALF + k * NARROW, half * HALF + (k + 1) * NARROW)
                h_out[m, :, at] = (
                    hid[m, :, at].astype(F32) + added[k * tokens:(k + 1) * tokens]
                ).astype(BF16)

            @pl.when(section < sections - 1)
            def _():
                relay_copy(m, half).start()

            @pl.when(section == sections - 1)
            def _():
                for to in range(2 * half, min(2 * half + 2, sections - 1)):
                    out_copy(m, to).start()
                if half == 1:
                    out_stay(m).start()

    def step(t, carry):
        u = t - AHEAD

        @pl.when(t == AHEAD)
        def _():
            for copy in weight_copies:
                copy.wait()
            swap_copy.wait_recv()

        @pl.when((t >= AHEAD) & (t < units + AHEAD))
        def _():
            compute(jnp.maximum(u, 0))

        @pl.when((lax.rem(t, 2) == core) & (t < units))
        def _():
            dispatch(t // 2)

        @pl.when((t >= AHEAD + BEHIND) & (lax.rem(t + 8 - AHEAD - BEHIND, 2) == core))
        def _():
            combine((jnp.maximum(t, AHEAD + BEHIND) - AHEAD - BEHIND) // 2)

        return carry

    lax.fori_loop(0, units + AHEAD + BEHIND, step, 0)

    def drain(m, carry):
        def drain_dispatch(step, inner):
            to = lax.rem(chip + step, CHIPS)
            dispatch_copy(m, to // 2, to, chip).wait_send()
            return inner

        lax.fori_loop(1, CHIPS, drain_dispatch, 0)

        @pl.when(side != core)
        def _():
            dispatch_copy(m, chip // 2, chip, chip).wait_send()

        for half in range(2):
            u = 2 * m + half
            for part in range(2):
                between_copy(u, part).wait_send()

            def drain_forward(k, inner, u=u):
                forward_copy(u, core * SOURCES + k).wait_send()
                return inner

            lax.fori_loop(0, SOURCES, drain_forward, 0)

            def drain_return(home, inner, u=u):
                @pl.when(jnp.logical_not(stays(u, home)))
                def _():
                    return_copy(u, home).wait_send()

                return inner

            lax.fori_loop(0, CHIPS, drain_return, 0)

        @pl.when(section < sections - 1)
        def _():
            for half in range(2):
                relay_copy(m, half).wait_send()

        @pl.when(section == sections - 1)
        def _():
            for to in range(sections - 1):
                out_copy(m, to).wait_send()

        out_stay(m).wait()
        return carry

    swap_copy.wait_send()
    lax.fori_loop(0, micros, drain, 0)


def on_device(inputs, routes, norm_gain, router, w_gate, w_up, w_down):
    micros, tokens, features = inputs.shape
    units = 2 * micros
    hidden_units = w_gate.shape[2]
    vmem = pl.BlockSpec(memory_space=pltpu.VMEM)
    anywhere = pl.BlockSpec(memory_space=pl.ANY)
    dma = pltpu.SemaphoreType.DMA
    return pl.pallas_call(
        kernel,
        out_shape=jax.ShapeDtypeStruct((micros, tokens, features // 4), BF16),
        in_specs=[anywhere, vmem, vmem, vmem] + [anywhere] * 3,
        out_specs=vmem,
        scratch_shapes=[
            pltpu.VMEM((hidden_units, features), BF16),
            pltpu.VMEM((hidden_units, features), BF16),
            pltpu.VMEM((2, hidden_units, HALF), BF16),
            pltpu.VMEM((PIECES * PACKED, SOURCES * BLOCK), BF16),
            pltpu.VMEM((SOURCES * BLOCK, PIECES * PACKED), BF16),
            pltpu.VMEM((micros, tokens, features), BF16),
            pltpu.VMEM((8 * BLOCK, PIECES * tokens), BF16),
            pltpu.VMEM((micros, 8 * BLOCK, WIDE), BF16),
            pltpu.VMEM((units, CHIPS, BLOCK, WIDE), BF16),
            pltpu.VMEM((2 * PACKED, features), BF16),
            pltpu.VMEM((units, 2 * PACKED, hidden_units), BF16),
            pltpu.VMEM((units, 2 * PACKED, hidden_units), BF16),
            pltpu.VMEM((2 * PACKED, HALF), F32),
            pltpu.VMEM((2, PIECES * PACKED, NARROW), BF16),
            pltpu.VMEM((units, CHIPS, BLOCK, NARROW), BF16),
            pltpu.VMEM((micros, 2, CHIPS, BLOCK, NARROW), BF16),
            pltpu.VMEM((2, PIECES * tokens, CHIPS * BLOCK), BF16),
            pltpu.VMEM((2, PIECES * tokens, CHIPS * BLOCK), BF16),
            pltpu.VMEM((micros, tokens, features), BF16),
            dma((4,)),
            dma((micros,)),
            dma((units, CHIPS)),
            dma((units,)),
            dma((micros, 2, CHIPS)),
            dma((micros,)),
            dma, dma, dma, dma, dma, dma,
        ],
        compiler_params=pltpu.CompilerParams(
            collective_id=0, has_side_effects=True, vmem_limit_bytes=60 * 2**20
        ),
        name="moe_relay",
    )(
        inputs, jnp.swapaxes(routes[0], 1, 2), norm_gain, router[0].T, w_gate[0].T, w_up[0].T,
        w_down[0],
    )


def solution(mesh):
    return jax.shard_map(
        on_device,
        mesh=mesh,
        in_specs=(
            P(None, "expert", None),
            P("section", None, "expert", None),
            P("section", None),
            P("section", None, None),
            P("section", None, "expert"),
            P("section", None, "expert"),
            P("section", "expert", None),
        ),
        out_specs=P(None, "expert", "section"),
        check_vma=False,
    )
```

time: 328 us -> 253 us (0.77)
  Pallas kernels: 308 us -> 250 us
  local copies, waits for them, and re-layouts: 19.6 us -> 1.65 us
    pallas_call x1, Pallas kernels: 308 us -> 250 us  [on_device(): pl.pallas_call(kernel, out_shape=jax.ShapeDtypeStruct((micros, tokens, fe...]
    unnamed x7 -> x1, local copies, waits for them, and re-layouts: 18.8 us -> 1.65 us
where the time goes in v2:
time: 253 us; the launch traced here: 252 us
  Pallas kernels  250 us (99%)
    pallas_call x1, Pallas kernels, on_device(): pl.pallas_call(kernel, out_shape=jax.ShapeDtypeStruct((micros, tokens, fe...  250 us

profile of v2, /device:TPU:1, one launch (start us, length us, event | category | flops | bytes accessed | tf_op | source)
XLA Modules:
  0.0 251.7 jit_solution(1786897808685302425)
XLA Ops:
  0.0 250.0 %moe_relay.1 = bf16[4,32,896]{2,1,0:T(8,128)(2,1)} custom-call(bf16[4,32,3584]{2,1,0:T(8,128)(2,1)} %inputs.1, s32[4,2,32]{2,1,0:T(2,128)} %bitcast.17, bf16[1,3584]{1,0:T(2,128)(2,1)} %gain.1, bf16[8,3584]{1,0:T(8,128)(2,1)} %bitcast.16, bf16[608,3584]{1,0:T(8,128)(2,1)} %bitcast.13, bf16[608,3584]{1,0:T(8,128)(2,1)} %bitcast.14, bf16[608,3584]{1,0:T(8,128)(2,1)} %bitcast.15), custom_call_target="tpu_custom_call" | custom-call | tf_op jit(solution)/shard_map/moe_relay/pallas_call | solution.py:432
  250.1 1.6 copy.9

commit v3 on v0

v3 whole, which is shorter than its diff:
```python
import jax
import jax.numpy as jnp
from jax import lax
from jax.experimental import pallas as pl
from jax.experimental.pallas import tpu as pltpu
from jax.sharding import PartitionSpec as P

EPSILON = 1e-06
MESH = pl.DeviceIdType.MESH
F32 = jnp.float32
BF16 = jnp.bfloat16

CAP = 9
HALF = 1792
PIECES = 7
NARROW = 256
BLOCK = 64
SOURCES = 8
PACKED = 80
CHIPS = 16
GROUP = 4
SLICE = 896
LANES = 128
STEPS = [
    (2, 2), (2, 1), (1, 2), (2, 3), (3, 2), (2, 0), (0, 2), (1, 1), (3, 3), (1, 3), (3, 1),
    (1, 0), (0, 1), (3, 0), (0, 3),
]


def fill_selection(sel, unsel):
    down = lax.broadcasted_iota(jnp.int32, (PIECES * PACKED, 1), 0)
    piece, rest = down // PACKED, lax.rem(down, PACKED)
    source, slot = rest // CAP, lax.rem(rest, CAP)
    taken = jnp.where(rest < SOURCES * CAP, source * BLOCK + piece * CAP + slot, -1)
    sel[...] = jnp.where(
        lax.broadcasted_iota(jnp.int32, sel.shape, 1) == taken, 1.0, 0.0
    ).astype(BF16)
    down = lax.broadcasted_iota(jnp.int32, (SOURCES * BLOCK, 1), 0)
    source, rest = down // BLOCK, lax.rem(down, BLOCK)
    piece, slot = rest // CAP, lax.rem(rest, CAP)
    taken = jnp.where(piece < PIECES, piece * PACKED + source * CAP + slot, -1)
    unsel[...] = jnp.where(
        lax.broadcasted_iota(jnp.int32, unsel.shape, 1) == taken, 1.0, 0.0
    ).astype(BF16)


def dot(rows, columns):
    return jnp.dot(rows, columns, preferred_element_type=F32)


def dot_nt(rows, columns):
    return lax.dot_general(
        rows, columns, (((1,), (1,)), ((), ())), preferred_element_type=F32
    )


def kernel(
    inputs, routes, gain, router, gate_in, up_in, down_in,
    out,
    w_gate, w_up, w_down, sel, unsel, routes_other, hid, square_first, square_out, squares,
    placing, d_out, held, packed, mid_out, mid_in, partial, answers, ret_out, came,
    diff_out, diff_in, weight_hi, weight_lo, h_out,
    w_sem, r_sem, h_sem, q_sem, d_sem, f_sem, mid_sem, ret_sem, diff_sem, out_sem,
    swap_sent, route_sent, input_sent, first_sent, d_sent, f_sent, mid_sent, ret_sent,
    diff_sent, h_sent, q_sent,
):
    micros, tokens, _ = inputs.shape
    units = 2 * micros
    section = lax.axis_index("section")
    place = lax.axis_index("expert")
    sections = 4
    core = lax.rem(place, 2)
    chip = place // 2
    x, y = chip // 4, lax.rem(chip, 4)
    sibling = (section, chip * 2 + (1 - core))
    onward = lax.rem(section + 1, sections)

    def remote(src, dst, sent, arrived, device):
        return pltpu.make_async_remote_copy(
            src, dst, sent, arrived, device_id=device, device_id_type=MESH
        )

    def landing(ref, arrived):
        return pltpu.make_async_copy(ref, ref, arrived)

    def columns_of(half):
        return pl.ds(pl.multiple_of(half * HALF, HALF), HALF)

    mine, others = columns_of(core), columns_of(1 - core)
    around = [(lax.rem(x + dx, 4) * 4 + lax.rem(y + dy, 4)) for dx, dy in STEPS]

    weight_copies = [
        pltpu.make_async_copy(gate_in.at[:, mine], w_gate.at[0], w_sem.at[0]),
        pltpu.make_async_copy(up_in.at[:, mine], w_up.at[0], w_sem.at[1]),
        pltpu.make_async_copy(gate_in.at[:, others], w_gate.at[1], w_sem.at[2]),
        pltpu.make_async_copy(up_in.at[:, others], w_up.at[1], w_sem.at[3]),
        pltpu.make_async_copy(down_in.at[:, mine], w_down.at[0], w_sem.at[4]),
    ]
    swap_copy = remote(down_in.at[:, others], w_down.at[1], swap_sent, w_sem.at[5], sibling)
    route_copy = remote(routes, routes_other, route_sent, r_sem, sibling)

    def input_stay(m):
        u = 2 * m + core
        return pltpu.make_async_copy(inputs.at[m, :, mine], hid.at[u], h_sem.at[u])

    def input_copy(m):
        u = 2 * m + core
        return remote(inputs.at[m, :, others], hid.at[u], input_sent, h_sem.at[u], sibling)

    @pl.when(section == 0)
    def _():
        for m in range(micros):
            input_stay(m).start()

    barrier = pltpu.get_barrier_semaphore()

    def greet(device):
        pl.semaphore_signal(barrier, inc=1, device_id=device, device_id_type=MESH)

    greet(sibling)
    for to in around:
        greet((section, to * 2 + core))
    for step in range(1, sections):
        for half in range(2):
            greet((lax.rem(section + step, sections), chip * 2 + half))
    for copy in weight_copies:
        copy.start()
    fill_selection(sel, unsel)
    pl.semaphore_wait(barrier, 1 + len(STEPS) + 2 * (sections - 1))
    route_copy.start()

    def sum_squares(values):
        total = jnp.sum(values * values, axis=-1, keepdims=True)
        return jnp.broadcast_to(total, (tokens, LANES))

    def first_stay(u):
        return pltpu.make_async_copy(
            square_first.at[u], squares.at[u, core], q_sem.at[u, core]
        )

    def first_copy(u):
        return remote(
            square_first.at[u], squares.at[u, core], first_sent, q_sem.at[u, core], sibling
        )

    @pl.when(section == 0)
    def _():
        for m in range(micros):
            input_copy(m).start()

        def first(u, carry):
            landing(hid.at[u], h_sem.at[u]).wait()
            square_first[u] = sum_squares(hid[u].astype(F32))
            first_copy(u).start()
            first_stay(u).start()
            return carry

        lax.fori_loop(0, units, first, 0)

    swap_copy.start()
    route_copy.wait_recv()

    def total(condition, axis):
        return jnp.sum(jnp.where(condition, 1, 0), axis=axis, keepdims=True)

    def grids():
        width = PIECES * tokens
        up_down = lax.broadcasted_iota(jnp.int32, (tokens, width), 0)
        left_right = lax.broadcasted_iota(jnp.int32, (tokens, width), 1)
        return up_down, left_right, lax.rem(left_right, tokens)

    def choices(u):
        up_down, left_right, token_of = grids()
        here = lax.rem(u, 2) == core
        chosen = jnp.where(here, routes[u // 2], routes_other[u // 2])
        square = up_down[:, :tokens] == left_right[:, :tokens]
        first = jnp.sum(jnp.where(square, chosen[0:1], 0), axis=1, keepdims=True)
        second = jnp.sum(jnp.where(square, chosen[1:2], 0), axis=1, keepdims=True)
        repeat = up_down == token_of
        first_row = jnp.sum(jnp.where(repeat, first, 0), axis=0, keepdims=True)
        second_row = jnp.sum(jnp.where(repeat, second, 0), axis=0, keepdims=True)
        return first, second, first_row, second_row

    def dispatch_copy(u, to):
        return remote(
            d_out.at[u, pl.ds(pl.multiple_of(to // 2 * BLOCK, BLOCK), BLOCK)],
            held.at[u, core, chip], d_sent, d_sem.at[u, chip], (section, to * 2 + core),
        )

    def dispatch_stay(u):
        return pltpu.make_async_copy(
            d_out.at[u, pl.ds(pl.multiple_of(chip // 2 * BLOCK, BLOCK), BLOCK)],
            held.at[u, core, chip], d_sem.at[u, chip],
        )

    def diff_copy(u):
        return remote(diff_out.at[u], diff_in.at[u], diff_sent, diff_sem.at[u], sibling)

    def dispatch(u):
        first, second, first_row, second_row = choices(u)
        up_down, left_right, token_of = grids()
        earlier = up_down < token_of
        slot_first = total((first == first_row) & earlier, 0)
        slot_second = total(first == second_row, 0) + total((second == second_row) & earlier, 0)
        width = PIECES * tokens
        piece_row = lax.broadcasted_iota(jnp.int32, (1, width), 1) // tokens * CAP
        target_first = first_row * BLOCK + piece_row + slot_first
        target_second = second_row * BLOCK + piece_row + slot_second
        rows = lax.broadcasted_iota(jnp.int32, (8 * BLOCK, width), 0)
        placing[...] = jnp.where(
            (rows == target_first) | (rows == target_second), 1.0, 0.0
        ).astype(BF16)

        @pl.when(section > 0)
        def _():
            landing(hid.at[u], h_sem.at[u]).wait()

        for half in range(2):
            landing(squares.at[u, half], q_sem.at[u, half]).wait()
        meansq = (squares[u, 0, :, 0:1] + squares[u, 1, :, 0:1]) * (1.0 / (2 * HALF))
        normed = (
            hid[u].astype(F32) * lax.rsqrt(meansq + EPSILON) * gain[:, mine].astype(F32)
        ).astype(BF16)
        stacked = jnp.concatenate(
            [normed[:, k * NARROW:(k + 1) * NARROW] for k in range(PIECES)], axis=0
        )
        d_out[u] = dot(placing[...], stacked).astype(BF16)
        for to in around:
            dispatch_copy(u, to).start()
        dispatch_stay(u).start()

        logits = dot_nt(normed, router[:, mine])
        expert_range = lax.broadcasted_iota(jnp.int32, logits.shape, 1)
        sign = jnp.where(first == expert_range, 1.0, 0.0) - jnp.where(
            second == expert_range, 1.0, 0.0
        )
        diff_out[u] = jnp.broadcast_to(
            jnp.sum(sign * logits, axis=1, keepdims=True), (tokens, LANES)
        )
        diff_copy(u).start()

    def weigh(u):
        first, second, first_row, second_row = choices(u)
        up_down, left_right, _ = grids()
        before = (left_right < up_down) & (left_right < tokens)
        own_first = total((first == first_row) & before, 1)
        own_second = total((second == first_row) & (left_right < tokens), 1) + total(
            (second == second_row) & before, 1
        )
        at_first = first * BLOCK + own_first
        at_second = second * BLOCK + own_second
        landing(diff_in.at[u], diff_sem.at[u]).wait()
        difference = diff_out[u][:, 0:1] + diff_in[u][:, 0:1]
        first_weight = 1.0 / (1.0 + jnp.exp(-difference))
        second_weight = 1.0 - first_weight
        column = lax.broadcasted_iota(jnp.int32, (tokens, CHIPS * BLOCK), 1)
        column = column // (2 * BLOCK) * BLOCK + lax.rem(column, BLOCK)
        for k in range(PIECES):
            weights = jnp.where(column == at_first + k * CAP, first_weight, 0.0) + jnp.where(
                column == at_second + k * CAP, second_weight, 0.0
            )
            high = weights.astype(BF16)
            weight_hi[k * tokens:(k + 1) * tokens, :] = high
            weight_lo[k * tokens:(k + 1) * tokens, :] = (weights - high.astype(F32)).astype(BF16)

    def forward_copy(u, half, group):
        at = pl.ds(group * GROUP, GROUP)
        return remote(
            held.at[u, half, at], held.at[u, half, at], f_sent, f_sem.at[u, group], sibling
        )

    def pass_on(u):
        for group in range(CHIPS // GROUP):
            for k in range(group * GROUP, (group + 1) * GROUP):
                landing(held.at[u, core, k], d_sem.at[u, k]).wait()
            forward_copy(u, core, group).start()

    def between_copy(u):
        return remote(mid_out.at[u], mid_in.at[u], mid_sent, mid_sem.at[u], sibling)

    def return_copy(u, home):
        return remote(
            ret_out.at[u, home], came.at[u, chip], ret_sent, ret_sem.at[u, chip],
            (section, home * 2 + core),
        )

    def return_stay(u):
        return pltpu.make_async_copy(
            ret_out.at[u, chip], came.at[u, chip], ret_sem.at[u, chip]
        )

    def pack(u, half, slot):
        for group in range(2):
            blocks = held[u, half, group * SOURCES:(group + 1) * SOURCES]
            chosen = dot(sel[...], blocks.reshape(SOURCES * BLOCK, NARROW)).astype(BF16)
            for k in range(PIECES):
                packed[
                    slot, group * PACKED:(group + 1) * PACKED, k * NARROW:(k + 1) * NARROW
                ] = chosen[k * PACKED:(k + 1) * PACKED]

    def compute(u):
        pack(u, core, 0)
        gated = dot_nt(packed[0], w_gate[0])
        upward = dot_nt(packed[0], w_up[0])
        for group in range(CHIPS // GROUP):
            landing(
                held.at[u, 1 - core, pl.ds(group * GROUP, GROUP)], f_sem.at[u, group]
            ).wait()
        pack(u, 1 - core, 1)
        gated = gated + dot_nt(packed[1], w_gate[1])
        upward = upward + dot_nt(packed[1], w_up[1])
        between = (gated / (1.0 + jnp.exp(-gated)) * upward).astype(BF16)
        mid_out[u] = between
        between_copy(u).start()
        partial[...] = dot(between, w_down[0])
        between_copy(u).wait_recv()
        theirs = mid_in[u]
        for k in range(PIECES):
            at = slice(k * NARROW, (k + 1) * NARROW)
            part = (partial[:, at] + dot(theirs, w_down[1, :, at])).astype(BF16)
            answers[0, k * PACKED:(k + 1) * PACKED] = part[:PACKED]
            answers[1, k * PACKED:(k + 1) * PACKED] = part[PACKED:]
        for group in range(2):
            blocks = dot(unsel[...], answers[group]).astype(BF16)
            ret_out[u, group * SOURCES:(group + 1) * SOURCES] = blocks.reshape(
                SOURCES, BLOCK, NARROW
            )
        for home in around:
            return_copy(u, home).start()
        return_stay(u).start()

    def relay_copy(u):
        return remote(h_out.at[u], hid.at[u], h_sent, h_sem.at[u], (onward, place))

    def square_copy(u, half):
        return remote(
            square_out.at[u], squares.at[u, core], q_sent, q_sem.at[u, core],
            (onward, chip * 2 + half),
        )

    def out_copy(u, q):
        return remote(
            h_out.at[u, :, q * SLICE:(q + 1) * SLICE], out.at[u // 2], h_sent,
            out_sem.at[u // 2], (2 * core + q, chip * 2 + lax.rem(u, 2)),
        )

    def out_stay(u):
        return pltpu.make_async_copy(
            h_out.at[u, :, SLICE:2 * SLICE], out.at[u // 2], out_sem.at[u // 2]
        )

    def stays(u):
        return (core == 1) & (lax.rem(u, 2) == core)

    def combine(u):
        def arrive(k, carry):
            landing(came.at[u, k], ret_sem.at[u, k]).wait()
            return carry

        lax.fori_loop(0, CHIPS, arrive, 0)
        answered = came[u].reshape(CHIPS * BLOCK, NARROW)
        added = dot(weight_hi[...], answered) + dot(weight_lo[...], answered)
        for k in range(PIECES):
            at = slice(k * NARROW, (k + 1) * NARROW)
            h_out[u, :, at] = (
                hid[u, :, at].astype(F32) + added[k * tokens:(k + 1) * tokens]
            ).astype(BF16)

        @pl.when(section < sections - 1)
        def _():
            relay_copy(u).start()
            square_out[u] = sum_squares(h_out[u].astype(F32))
            for half in range(2):
                square_copy(u, half).start()

        @pl.when(section == sections - 1)
        def _():
            out_copy(u, 0).start()

            @pl.when(stays(u))
            def _():
                out_stay(u).start()

            @pl.when(jnp.logical_not(stays(u)))
            def _():
                out_copy(u, 1).start()

    def step(t, carry):
        u = jnp.maximum(t - 1, 0)
        working = (t >= 1) & (t <= units)

        @pl.when(working)
        def _():
            pass_on(u)

        @pl.when(t < units)
        def _():
            dispatch(t)

        @pl.when(t == 1)
        def _():
            for copy in weight_copies:
                copy.wait()
            swap_copy.wait_recv()

        @pl.when(working)
        def _():
            compute(u)

        @pl.when(t >= 2)
        def _():
            combine(jnp.maximum(t - 2, 0))

        @pl.when(working)
        def _():
            weigh(u)

        return carry

    lax.fori_loop(0, units + 2, step, 0)

    swap_copy.wait_send()
    route_copy.wait_send()

    @pl.when(section == 0)
    def _():
        for m in range(micros):
            input_copy(m).wait_send()

    def drain(u, carry):
        @pl.when(section == 0)
        def _():
            first_copy(u).wait_send()

        for to in around:
            dispatch_copy(u, to).wait_send()
            return_copy(u, to).wait_send()
        diff_copy(u).wait_send()
        for group in range(CHIPS // GROUP):
            forward_copy(u, core, group).wait_send()
        between_copy(u).wait_send()

        @pl.when(section < sections - 1)
        def _():
            relay_copy(u).wait_send()
            for half in range(2):
                square_copy(u, half).wait_send()

        @pl.when(section == sections - 1)
        def _():
            out_copy(u, 0).wait_send()

            @pl.when(jnp.logical_not(stays(u)))
            def _():
                out_copy(u, 1).wait_send()

        return carry

    lax.fori_loop(0, units, drain, 0)
    for m in range(micros):
        landing(out.at[m], out_sem.at[m]).wait()


def on_device(inputs, routes, norm_gain, router, w_gate, w_up, w_down):
    micros, tokens, features = inputs.shape
    units = 2 * micros
    hidden_units = w_gate.shape[2]
    vmem = pl.BlockSpec(memory_space=pltpu.VMEM)
    anywhere = pl.BlockSpec(memory_space=pl.ANY)
    dma = pltpu.SemaphoreType.DMA

    def bf16(*shape):
        return pltpu.VMEM(shape, BF16)

    def f32(*shape):
        return pltpu.VMEM(shape, F32)

    return pl.pallas_call(
        kernel,
        out_shape=jax.ShapeDtypeStruct((micros, tokens, SLICE), BF16),
        in_specs=[anywhere, vmem, vmem, vmem] + [anywhere] * 3,
        out_specs=vmem,
        scratch_shapes=[
            bf16(2, hidden_units, HALF),
            bf16(2, hidden_units, HALF),
            bf16(2, hidden_units, HALF),
            bf16(PIECES * PACKED, SOURCES * BLOCK),
            bf16(SOURCES * BLOCK, PIECES * PACKED),
            pltpu.VMEM((micros, 2, tokens), jnp.int32),
            bf16(units, tokens, HALF),
            f32(units, tokens, LANES),
            f32(units, tokens, LANES),
            f32(units, 2, tokens, LANES),
            bf16(8 * BLOCK, PIECES * tokens),
            bf16(units, 8 * BLOCK, NARROW),
            bf16(units, 2, CHIPS, BLOCK, NARROW),
            bf16(2, 2 * PACKED, HALF),
            bf16(units, 2 * PACKED, hidden_units),
            bf16(units, 2 * PACKED, hidden_units),
            f32(2 * PACKED, HALF),
            bf16(2, PIECES * PACKED, NARROW),
            bf16(units, CHIPS, BLOCK, NARROW),
            bf16(units, CHIPS, BLOCK, NARROW),
            f32(units, tokens, LANES),
            f32(units, tokens, LANES),
            bf16(PIECES * tokens, CHIPS * BLOCK),
            bf16(PIECES * tokens, CHIPS * BLOCK),
            bf16(units, tokens, HALF),
            dma((6,)),
            dma,
            dma((units,)),
            dma((units, 2)),
            dma((units, CHIPS)),
            dma((units, CHIPS // GROUP)),
            dma((units,)),
            dma((units, CHIPS)),
            dma((units,)),
            dma((micros,)),
        ] + [dma] * 11,
        compiler_params=pltpu.CompilerParams(
            collective_id=0, has_side_effects=True, vmem_limit_bytes=60 * 2**20
        ),
        name="moe_relay",
    )(
        inputs, jnp.swapaxes(routes[0], 1, 2), norm_gain, router[0].T, w_gate[0].T, w_up[0].T,
        w_down[0],
    )


def solution(mesh):
    return jax.shard_map(
        on_device,
        mesh=mesh,
        in_specs=(
            P(None, "expert", None),
            P("section", None, "expert", None),
            P("section", None),
            P("section", None, None),
            P("section", None, "expert"),
            P("section", None, "expert"),
            P("section", "expert", None),
        ),
        out_specs=P(None, "expert", "section"),
        check_vma=False,
    )
```

time: 1040 us -> 236 us (0.23)
  blocking collectives: 372 us -> 0 us
  waiting for transfers between devices: 362 us -> 0 us
  Pallas kernels: 0 us -> 234 us
  matrix products: 103 us -> 0 us
  local copies, waits for them, and re-layouts: 87.5 us -> 1.65 us
  starting transfers between devices: 56.7 us -> 0 us
  other arithmetic: 34.9 us -> 0 us
  between operations: 14.5 us -> 0.01 us
    all_to_all x7 -> x0, blocking collectives: 372 us -> none  [expert_pass(): lax.all_to_all(outgoing, 'expert', split_axis=0, concat_axis=0, tiled=True)]
    all_to_all x7 -> x0, waiting for transfers between devices: 315 us -> none  [expert_pass(): lax.all_to_all(answered, 'expert', split_axis=0, concat_axis=0, tiled=True)]
    pallas_call x0 -> x1, Pallas kernels: none -> 234 us  [on_device(): pl.pallas_call(kernel, out_shape=jax.ShapeDtypeStruct((micros, tokens, SL...]
    dot_general x28 -> x0, matrix products: 103 us -> none  [the longest x7 66.9 us: expert_block(): jnp.dot(between, down_block, preferred_element_type=jnp.float32)]
    reshape x28 -> x0, local copies, waits for them, and re-layouts: 62.4 us -> none  [the longest x7 30.9 us: expert_pass(): answered = answered.reshape(sources, item_count, width)]
    all_to_all x7 -> x0, starting transfers between devices: 32.5 us -> none  [expert_pass(): lax.all_to_all(answered, 'expert', split_axis=0, concat_axis=0, tiled=True)]
    reduce_sum x21 -> x0, other arithmetic: 25.8 us -> none  [the longest x7 20.5 us: expert_pass(): combined = jnp.sum(combined, axis=1).reshape(slots_total, feature_count)]
    ppermute x6 -> x0, starting transfers between devices: 24.1 us -> none  [from_behind(): return lax.ppermute(array, axis, pairs)]
  transfers between devices with their start and end apart: 14 -> 0, of which waited for: 14 -> 0; matrix products, arithmetic and copies ran while one was open for 1% -> 0% of each run, Pallas kernels for 0% -> 0%
where the time goes in v3:
time: 236 us
  Pallas kernels  234 us (99%)
    pallas_call x1, Pallas kernels, on_device(): pl.pallas_call(kernel, out_shape=jax.ShapeDtypeStruct((micros, tokens, SL...  234 us

profile of v3, /device:TPU:1, one launch (start us, length us, event | category | flops | bytes accessed | tf_op | source)
XLA Modules:
  0.0 236.1 jit_solution(1193244839071765999)
XLA Ops:
  0.0 234.5 %moe_relay.1 = bf16[4,32,896]{2,1,0:T(8,128)(2,1)} custom-call(bf16[4,32,3584]{2,1,0:T(8,128)(2,1)} %inputs.1, s32[4,2,32]{2,1,0:T(2,128)} %bitcast.17, bf16[1,3584]{1,0:T(2,128)(2,1)} %gain.1, bf16[8,3584]{1,0:T(8,128)(2,1)} %bitcast.16, bf16[608,3584]{1,0:T(8,128)(2,1)} %bitcast.13, bf16[608,3584]{1,0:T(8,128)(2,1)} %bitcast.14, bf16[608,3584]{1,0:T(8,128)(2,1)} %bitcast.15), custom_call_target="tpu_custom_call" | custom-call | tf_op jit(solution)/shard_map/moe_relay/pallas_call | solution.py:478
  234.5 1.6 copy.9

commit v4 on v3

--- a/solution.py
+++ b/solution.py
@@ -57,7 +57,7 @@
 def kernel(
     inputs, routes, gain, router, gate_in, up_in, down_in,
     out,
-    w_gate, w_up, w_down, sel, unsel, routes_other, hid, square_first, square_out, squares,
+    w_gate, w_up, w_gate_turned, w_up_turned, w_down, sel, unsel, routes_other, hid, square_first, square_out, squares,
     placing, d_out, held, packed, mid_out, mid_in, partial, answers, ret_out, came,
     diff_out, diff_in, weight_hi, weight_lo, h_out,
     w_sem, r_sem, h_sem, q_sem, d_sem, f_sem, mid_sem, ret_sem, diff_sem, out_sem,
@@ -300,15 +300,15 @@
 
     def compute(u):
         pack(u, core, 0)
-        gated = dot_nt(packed[0], w_gate[0])
-        upward = dot_nt(packed[0], w_up[0])
+        gated = dot(packed[0], w_gate_turned[0])
+        upward = dot(packed[0], w_up_turned[0])
         for group in range(CHIPS // GROUP):
             landing(
                 held.at[u, 1 - core, pl.ds(group * GROUP, GROUP)], f_sem.at[u, group]
             ).wait()
         pack(u, 1 - core, 1)
-        gated = gated + dot_nt(packed[1], w_gate[1])
-        upward = upward + dot_nt(packed[1], w_up[1])
+        gated = gated + dot(packed[1], w_gate_turned[1])
+        upward = upward + dot(packed[1], w_up_turned[1])
         between = (gated / (1.0 + jnp.exp(-gated)) * upward).astype(BF16)
         mid_out[u] = between
         between_copy(u).start()
@@ -385,6 +385,23 @@
             def _():
                 out_copy(u, 1).start()
 
+    def turn():
+        for copy in weight_copies:
+            copy.wait()
+
+        def turn_columns(k, carry):
+            at = pl.ds(pl.multiple_of(k * LANES, LANES), LANES)
+            for half in range(2):
+                w_gate_turned[half, at, :] = w_gate[half, :, at].T
+                w_up_turned[half, at, :] = w_up[half, :, at].T
+            return carry
+
+        lax.fori_loop(0, HALF // LANES, turn_columns, 0)
+
+    @pl.when(section > 0)
+    def _():
+        turn()
+
     def step(t, carry):
         u = jnp.maximum(t - 1, 0)
         working = (t >= 1) & (t <= units)
@@ -397,10 +414,12 @@
         def _():
             dispatch(t)
 
+        @pl.when((t == 0) & (section == 0))
+        def _():
+            turn()
+
         @pl.when(t == 1)
         def _():
-            for copy in weight_copies:
-                copy.wait()
             swap_copy.wait_recv()
 
         @pl.when(working)
@@ -483,6 +502,8 @@
         scratch_shapes=[
             bf16(2, hidden_units, HALF),
             bf16(2, hidden_units, HALF),
+            bf16(2, HALF, hidden_units),
+            bf16(2, HALF, hidden_units),
             bf16(2, hidden_units, HALF),
             bf16(PIECES * PACKED, SOURCES * BLOCK),
             bf16(SOURCES * BLOCK, PIECES * PACKED),

time: 236 us -> 230 us (0.975)
  Pallas kernels: 234 us -> 228 us
    pallas_call x1, Pallas kernels: 234 us -> 228 us  [on_device(): pl.pallas_call(kernel, out_shape=jax.ShapeDtypeStruct((micros, tokens, SL...]
where the time goes in v4:
time: 230 us
  Pallas kernels  228 us (99%)
    pallas_call x1, Pallas kernels, on_device(): pl.pallas_call(kernel, out_shape=jax.ShapeDtypeStruct((micros, tokens, SL...  228 us

profile of v4, /device:TPU:1, one launch (start us, length us, event | category | flops | bytes accessed | tf_op | source)
XLA Modules:
  0.0 229.7 jit_solution(1082015444299379192)
XLA Ops:
  0.0 228.0 %moe_relay.1 = bf16[4,32,896]{2,1,0:T(8,128)(2,1)} custom-call(bf16[4,32,3584]{2,1,0:T(8,128)(2,1)} %inputs.1, s32[4,2,32]{2,1,0:T(2,128)} %bitcast.17, bf16[1,3584]{1,0:T(2,128)(2,1)} %gain.1, bf16[8,3584]{1,0:T(8,128)(2,1)} %bitcast.16, bf16[608,3584]{1,0:T(8,128)(2,1)} %bitcast.13, bf16[608,3584]{1,0:T(8,128)(2,1)} %bitcast.14, bf16[608,3584]{1,0:T(8,128)(2,1)} %bitcast.15), custom_call_target="tpu_custom_call" | custom-call | tf_op jit(solution)/shard_map/moe_relay/pallas_call | solution.py:497
  228.0 1.6 copy.9

commit v5 on v4

--- a/solution.py
+++ b/solution.py
@@ -59,7 +59,7 @@
     out,
     w_gate, w_up, w_gate_turned, w_up_turned, w_down, sel, unsel, routes_other, hid, square_first, square_out, squares,
     placing, d_out, held, packed, mid_out, mid_in, partial, answers, ret_out, came,
-    diff_out, diff_in, weight_hi, weight_lo, h_out,
+    diff_out, diff_in, weights, h_out,
     w_sem, r_sem, h_sem, q_sem, d_sem, f_sem, mid_sem, ret_sem, diff_sem, out_sem,
     swap_sent, route_sent, input_sent, first_sent, d_sent, f_sent, mid_sent, ret_sent,
     diff_sent, h_sent, q_sent,
@@ -256,12 +256,11 @@
         column = lax.broadcasted_iota(jnp.int32, (tokens, CHIPS * BLOCK), 1)
         column = column // (2 * BLOCK) * BLOCK + lax.rem(column, BLOCK)
         for k in range(PIECES):
-            weights = jnp.where(column == at_first + k * CAP, first_weight, 0.0) + jnp.where(
-                column == at_second + k * CAP, second_weight, 0.0
-            )
-            high = weights.astype(BF16)
-            weight_hi[k * tokens:(k + 1) * tokens, :] = high
-            weight_lo[k * tokens:(k + 1) * tokens, :] = (weights - high.astype(F32)).astype(BF16)
+            weights[k * tokens:(k + 1) * tokens, :] = jnp.where(
+                column == at_first + k * CAP,
+                first_weight,
+                jnp.where(column == at_second + k * CAP, second_weight, 0.0),
+            ).astype(BF16)
 
     def forward_copy(u, half, group):
         at = pl.ds(group * GROUP, GROUP)
@@ -359,7 +358,7 @@
 
         lax.fori_loop(0, CHIPS, arrive, 0)
         answered = came[u].reshape(CHIPS * BLOCK, NARROW)
-        added = dot(weight_hi[...], answered) + dot(weight_lo[...], answered)
+        added = dot(weights[...], answered)
         for k in range(PIECES):
             at = slice(k * NARROW, (k + 1) * NARROW)
             h_out[u, :, at] = (
@@ -525,7 +524,6 @@
             f32(units, tokens, LANES),
             f32(units, tokens, LANES),
             bf16(PIECES * tokens, CHIPS * BLOCK),
-            bf16(PIECES * tokens, CHIPS * BLOCK),
             bf16(units, tokens, HALF),
             dma((6,)),
             dma,

time: 230 us -> 232 us (level)
  no operation moved by 1% of the time
where the time goes in v5:
time: 232 us; the launch traced here: 231 us
  Pallas kernels  230 us (99%)
    pallas_call x1, Pallas kernels, on_device(): pl.pallas_call(kernel, out_shape=jax.ShapeDtypeStruct((micros, tokens, SL...  230 us

profile of v5, /device:TPU:1, one launch (start us, length us, event | category | flops | bytes accessed | tf_op | source)
XLA Modules:
  0.0 231.3 jit_solution(6438372333130197538)
XLA Ops:
  0.0 229.7 %moe_relay.1 = bf16[4,32,896]{2,1,0:T(8,128)(2,1)} custom-call(bf16[4,32,3584]{2,1,0:T(8,128)(2,1)} %inputs.1, s32[4,2,32]{2,1,0:T(2,128)} %bitcast.17, bf16[1,3584]{1,0:T(2,128)(2,1)} %gain.1, bf16[8,3584]{1,0:T(8,128)(2,1)} %bitcast.16, bf16[608,3584]{1,0:T(8,128)(2,1)} %bitcast.13, bf16[608,3584]{1,0:T(8,128)(2,1)} %bitcast.14, bf16[608,3584]{1,0:T(8,128)(2,1)} %bitcast.15), custom_call_target="tpu_custom_call" | custom-call | tf_op jit(solution)/shard_map/moe_relay/pallas_call | solution.py:496
  229.7 1.6 copy.9
